TPU v7x, 256 devices: a whole 4x4x8 slice. The times are simulated.
256 devices in a mesh: dp: 8 (over y, core), tm: 32 (over z, x).
Axes of the slice: x: 4, y: 4, z: 8, core: 2. Of those that a mesh axis runs over, the one named last changes fastest.
Arguments:
- frames: bfloat16 [65536, 1536], P(('dp', 'tm')), may hold values from -28 to 28, as said below
- seg: int32 [8, 8192], P('dp'), may hold values from 0 to 3, never falling along the last dimension, each value on 1 to 4096 neighbouring positions
- look_back: int32 [8, 32], P('dp'), may hold values 0 or 1
- w_dw: float32 [5, 1536], replicated, may hold values from -2.5 to 2.5
- w_qkv: bfloat16 [1536, 4608], P(None, 'dp'), may hold values from -0.15625 to 0.15625
- w_o: bfloat16 [1536, 1536], replicated, may hold values from -1.5 to 1.5
- cotangent: bfloat16 [65536, 1536], P(('dp', 'tm')), may hold values from -1 to 1
Outputs:
- mixed: bfloat16 [65536, 1536], P(('dp', 'tm'))
- weight_grad: float32 [1536, 1536], P('tm', 'dp')
Inputs may be any that keep to these rules, and one draw needn't show every extreme that they name: Float features; a few short runs of frames may be several times larger than the rest. `seg`: recording numbers never fall along a replica's frames; each recording has 1 to 4096 frames, one exactly 4096.
All inputs are finite; a program needn't handle non-finite values. No bound on the sum of `look_back` on one device may be relied on, other than what follows from the above.
Results may differ from a plain program's by a relative error of at most 0.012.
The roundings to bfloat16 on the way count: a program that leaves them out, or rounds other values in their place, can miss the bound.
Values may be sent and summed in bfloat16 or wider, within the bound.
A program may use at most 128 MiB of HBM per device.

v0:
```python
import math
import jax
import jax.numpy as jnp
from jax import lax
from jax.sharding import PartitionSpec as P

KER = 5
STRETCH = 256


def extended(block, sides, width):
    for axis, dim in sides:
        count = lax.axis_size(axis)
        forward = [(i, i + 1) for i in range(count - 1)]
        backward = [(target, source) for source, target in forward]
        low = lax.ppermute(
            lax.slice_in_dim(block, block.shape[dim] - width, None, axis=dim), axis, forward
        )
        high = lax.ppermute(lax.slice_in_dim(block, 0, width, axis=dim), axis, backward)
        block = jnp.concatenate([low, block, high], axis=dim)
    return block


def swapped(block, axis, distance):
    count = lax.axis_size(axis)
    route = []
    for low in range(count):
        high = low | 1 << distance
        if high != low and high < count:
            route += [(low, high), (high, low)]
    return lax.ppermute(block, axis, route)


def stretch_attention(queries, keys, values, seg_row, look_row, stretch):
    frame_count, heads_here, head_dim = queries.shape
    value_dim = values.shape[2]
    blocks = frame_count // stretch
    query_blocks = queries.reshape(blocks, stretch, heads_here, head_dim)
    key_blocks = keys.reshape(blocks, stretch, heads_here, head_dim)
    value_blocks = values.reshape(blocks, stretch, heads_here, value_dim)
    key_pairs = jnp.concatenate(
        [jnp.concatenate([jnp.zeros_like(key_blocks[:1]), key_blocks[:-1]], 0), key_blocks], 1
    )
    value_pairs = jnp.concatenate(
        [jnp.concatenate([jnp.zeros_like(value_blocks[:1]), value_blocks[:-1]], 0), value_blocks], 1
    )
    seg_blocks = seg_row.reshape(blocks, stretch)
    seg_pairs = jnp.concatenate(
        [jnp.concatenate([jnp.full((1, stretch), -1, jnp.int32), seg_blocks[:-1]], 0), seg_blocks],
        1,
    )
    allow_prev = look_row == 1
    per_step = math.gcd(blocks, max(1, 512 // stretch))
    current = jnp.arange(2 * stretch) >= stretch
    scale = 1.0 / math.sqrt(head_dim)

    def block_step(block_index):
        start = block_index * per_step

        def pick_rows(array):
            return lax.dynamic_slice_in_dim(array, start, per_step, 0)

        scores = (
            jnp.einsum(
                "gqhd,gkhd->ghqk",
                pick_rows(query_blocks),
                pick_rows(key_pairs),
                preferred_element_type=jnp.float32,
            )
            * scale
        )
        same_rec = pick_rows(seg_pairs)[:, None, :] == pick_rows(seg_blocks)[:, :, None]
        allowed = same_rec & (current[None, None, :] | pick_rows(allow_prev)[:, None, None])
        scores = jnp.where(allowed[:, None], scores, -1e30)
        row_max = jnp.max(scores, axis=-1, keepdims=True)
        raw_weights = jnp.exp(scores - row_max)
        probs = (raw_weights / jnp.sum(raw_weights, axis=-1, keepdims=True)).astype(jnp.bfloat16)
        outputs = jnp.einsum(
            "ghqk,gkhv->gqhv", probs, pick_rows(value_pairs), preferred_element_type=jnp.float32
        )
        return outputs.astype(jnp.bfloat16).reshape(per_step * stretch, heads_here * value_dim)

    mixed = lax.map(block_step, jnp.arange(blocks // per_step, dtype=jnp.int32))
    return mixed.reshape(frame_count, heads_here * value_dim)


def local(frames, seg, look_back, w_dw, w_qkv, w_o, cotangent):
    rows = frames.shape[0]
    width = frames.shape[1]
    tm_count = lax.axis_size("tm")
    piece = width // tm_count
    half = KER // 2
    padded = extended(frames, (("tm", 0),), half)
    seg_row = seg[0]
    look_row = look_back[0]
    seg_padded = jnp.pad(seg_row, (half, half), constant_values=-1)
    local_seg = lax.dynamic_slice_in_dim(
        seg_padded, lax.axis_index("tm") * rows, rows + 2 * half, 0
    )
    own_seg = local_seg[half : half + rows]
    total = jnp.zeros((rows, width), jnp.float32)
    for offset in range(KER):
        same_rec = (local_seg[offset : offset + rows] == own_seg).astype(jnp.float32)
        total = (
            total
            + w_dw[offset] * padded[offset : offset + rows].astype(jnp.float32) * same_rec[:, None]
        )
    activ = jax.nn.silu(total).astype(jnp.bfloat16)
    qkv = jnp.dot(
        activ, lax.all_gather(w_qkv, "dp", axis=1, tiled=True), preferred_element_type=jnp.float32
    ).astype(jnp.bfloat16)
    arranged = qkv.reshape(rows, 3, tm_count, piece)
    arrived = lax.all_to_all(arranged, "tm", split_axis=2, concat_axis=0, tiled=True)
    frame_count = arrived.shape[0]
    lower = lax.axis_index("tm") % 2 == 0
    own_pair = arrived[:, 0:2, 0, :]
    other_pair = swapped(own_pair, "tm", 0)
    joined = jnp.where(
        lower,
        jnp.concatenate([own_pair, other_pair], -1),
        jnp.concatenate([other_pair, own_pair], -1),
    )
    queries = joined[:, 0][:, None, :]
    keys = joined[:, 1][:, None, :]
    values = arrived[:, 2, 0, :][:, None, :]
    attended = stretch_attention(queries, keys, values, seg_row, look_row, STRETCH)
    returned = lax.all_to_all(
        attended.reshape(frame_count, 1, piece), "tm", split_axis=0, concat_axis=1, tiled=True
    )
    attn = returned.reshape(rows, width)
    mixed = jnp.dot(attn, w_o, preferred_element_type=jnp.float32).astype(jnp.bfloat16)
    grad_term = lax.dot_general(
        attn, cotangent, (((0,), (0,)), ((), ())), preferred_element_type=jnp.float32
    )
    row_share = lax.psum_scatter(grad_term, "tm", scatter_dimension=0, tiled=True)
    weight_grad = lax.psum_scatter(row_share, "dp", scatter_dimension=1, tiled=True)
    return (mixed, weight_grad)


def solution(mesh):
    placed = (
        P(("dp", "tm"), None),
        P("dp", None),
        P("dp", None),
        P(),
        P(None, "dp"),
        P(),
        P(("dp", "tm"), None),
    )
    return jax.shard_map(
        local,
        mesh=mesh,
        in_specs=placed,
        out_specs=(P(("dp", "tm"), None), P("tm", "dp")),
        check_vma=False,
    )
```

profile of v0, /device:TPU:4, one launch (start us, length us, event | category | flops | bytes accessed | tf_op | source)
XLA Modules:
  0.0 700.8 jit_solution(11983358287464709644)
XLA Ops:
  8.4 2.4 collective-permute-start.1
  10.9 3.4 collective-permute-start
  14.6 2.0 collective-permute-done
  16.6 72.7 %all-gather.2.cloned.1.call-done = bf16[1536,4608]{0,1:T(8,128)(2,1)} async-done(((bf16[1536,576]{0,1:T(8,128)(2,1)}), bf16[1536,4608]{0,1:T(8,128)(2,1)}) %all-gather.2.cloned.1.call-update) | async-done | bytes 14155792 | tf_op jit(solution)/shard_map/all_gather | solution.py:110
  89.4 11.5 %convolution_convert_fusion.1 = bf16[256,4608]{1,0:T(8,128)(2,1)} fusion(bf16[1536,4608]{0,1:T(8,128)(2,1)} %all-gather.2.cloned.1.call-done, bf16[256,1536]{1,0:T(8,128)(2,1)S(1)} %copy-done.4, bf16[2,1536]{1,0:T(2,128)(2,1)S(1)} %collective-permute-done, bf16[258,1536]{1,0:T(8,128)(2,1)S(1)} %constant_dynamic-update-slice_fusion.1, ...), kind=kOutput, calls=%fused_computation.23 | convolution fusion | flops 3636461568 | bytes 18925568 | tf_op jit(solution)/shard_map/dot_general | solution.py:109
  100.8 2.8 copy.24
  103.8 66.5 %all_to_all.33 = bf16[256,3,32,48]{0,3,1,2:T(8,128)(2,1)S(1)} all-to-all(bf16[256,3,32,48]{0,3,1,2:T(8,128)(2,1)S(1)} %copy.25), channel_id=1, replica_groups=mesh['dp'=8,'tm'=32] {'tm'}, dimensions={2} | all-to-all | bytes 4718592 | tf_op jit(solution)/shard_map/all_to_all | solution.py:113
  170.6 1.3 slice_bitcast_fusion
  171.9 1.3 collective-permute-start.2
  177.0 1.6 fusion.13
  178.6 29.1 %collective-permute-done.2 = bf16[8192,2,48]{0,2,1:T(8,128)(2,1)} collective-permute-done((bf16[8192,2,48]{0,2,1:T(8,128)(2,1)}, bf16[8192,2,48]{0,2,1:T(8,128)(2,1)}, u32[]{:S(2)}, u32[]{:S(2)}) %collective-permute-start.2) | collective-permute-done | bytes 1572896 | tf_op jit(solution)/shard_map/ppermute | solution.py:31
  207.6 3.8 maximum_select_fusion
  211.7 1.3 slice.119
  213.0 1.6 copy.44
  214.6 3.6 slice.109
  218.2 1.6 copy.43
  220.6 2.9 fusion.11
  223.5 98.1 %while.11 = (s32[]{:T(128)}, bf16[16,512,48]{1,2,0:T(8,128)(2,1)S(1)}, s32[16]{0:T(128)S(1)}, bf16[32,512,1,48]{1,0,3,2:T(8,128)(2,1)}, s32[32,512]{1,0:T(8,128)...) while((s32[]{:T(128)}, ...), condition=%wide.region_3.4_spmd.clone, body=%wide.region_0.3_spmd.clone.sunk | while | flops 77621248 | bytes 3646681 | solution.py:83
  224.7 1.3 constant_dynamic-slice_fusion.12
  226.1 1.1 constant_dynamic-slice_fusion.13
  228.0 1.1 constant_dynamic-slice_fusion.14
  230.9 1.3 constant_dynamic-slice_fusion.12
  232.2 1.1 constant_dynamic-slice_fusion.13
  237.0 1.3 constant_dynamic-slice_fusion.12
  238.3 1.1 constant_dynamic-slice_fusion.13
  243.1 1.3 constant_dynamic-slice_fusion.12
  244.5 1.1 constant_dynamic-slice_fusion.13
  249.3 1.3 constant_dynamic-slice_fusion.12
  250.6 1.1 constant_dynamic-slice_fusion.13
  255.4 1.3 constant_dynamic-slice_fusion.12
  256.7 1.1 constant_dynamic-slice_fusion.13
  261.5 1.3 constant_dynamic-slice_fusion.12
  262.9 1.1 constant_dynamic-slice_fusion.13
  267.7 1.3 constant_dynamic-slice_fusion.12
  269.0 1.1 constant_dynamic-slice_fusion.13
  273.8 1.3 constant_dynamic-slice_fusion.12
  275.1 1.1 constant_dynamic-slice_fusion.13
  279.9 1.3 constant_dynamic-slice_fusion.12
  281.3 1.1 constant_dynamic-slice_fusion.13
  286.1 1.3 constant_dynamic-slice_fusion.12
  287.4 1.1 constant_dynamic-slice_fusion.13
  292.2 1.3 constant_dynamic-slice_fusion.12
  293.5 1.1 constant_dynamic-slice_fusion.13
  298.3 1.3 constant_dynamic-slice_fusion.12
  299.7 1.1 constant_dynamic-slice_fusion.13
  304.5 1.3 constant_dynamic-slice_fusion.12
  305.8 1.1 constant_dynamic-slice_fusion.13
  310.6 1.3 constant_dynamic-slice_fusion.12
  311.9 1.1 constant_dynamic-slice_fusion.13
  316.7 1.3 constant_dynamic-slice_fusion.12
  318.1 1.1 constant_dynamic-slice_fusion.13
  322.5 2.0 copy.34
  324.5 6.2 reshape.89
  331.2 45.2 %reduce.20 = bf16[8192,48]{1,0:T(8,128)(2,1)S(1)} reduce(bf16[8192,1,48]{2,1,0:T(2,128)(2,1)} %reshape.89, bf16[]{:T(256)} %broadcast.84), dimensions={1}, to_apply=%reshape.89.reduce_sub_computation | reduce | bytes 1572866 | tf_op jit(solution)/shard_map/reshape;reshape | solution.py:128
  376.4 4.2 reshape.107
  380.6 27.1 %all_to_all.34 = bf16[32,2,6144]{2,1,0:T(2,128)(2,1)S(1)} all-to-all(bf16[32,2,6144]{2,1,0:T(2,128)(2,1)} %reshape.107), channel_id=1, replica_groups=mesh['dp'=8,'tm'=32] {'tm'}, dimensions={0} | all-to-all | bytes 1572864 | tf_op jit(solution)/shard_map/all_to_all | solution.py:127
  407.7 7.9 %reshape.108 = bf16[8192,1,48]{2,1,0:T(2,128)(2,1)} reshape(bf16[32,2,6144]{2,1,0:T(2,128)(2,1)S(1)} %all_to_all.34) | data formatting | bytes 1572864
  415.5 8.1 %copy.32 = bf16[8192,1,48]{0,2,1:T(8,128)(2,1)S(1)} copy(bf16[8192,1,48]{2,1,0:T(2,128)(2,1)} %reshape.108) | data formatting | bytes 1572864 | tf_op jit(solution)/shard_map/all_to_all | solution.py:127
  424.3 5.0 fusion.34
  429.4 227.5 %reduce-scatter.5.cloned.1.call-done = f32[48,1536]{1,0:T(8,128)} async-done(((f32[1536,1536]{1,0:T(8,128)}), f32[48,1536]{1,0:T(8,128)}) %reduce-scatter.5.cloned.1.call-update) | async-done | bytes 294928 | tf_op jit(solution)/shard_map/reduce_scatter | solution.py:135
  656.9 2.1 copy.35
  659.1 4.6 convolution_convert_fusion.2
  663.7 29.0 %reduce-scatter.7.cloned.1.call-done = f32[192,48]{1,0:T(8,128)} async-done(((f32[1536,48]{1,0:T(8,128)}), f32[192,48]{1,0:T(8,128)}) %reduce-scatter.7.cloned.1.call-update) | async-done | bytes 36880
  692.7 1.6 copy.36
  (243 shorter events, 54.9 us)
Async XLA Ops:
  7.2 417.1 %copy-start = (bf16[256,1536]{1,0:T(8,128)(2,1)S(1)}, bf16[256,1536]{1,0:T(8,128)(2,1)}, u32[]{:S(2)}) copy-start(bf16[256,1536]{1,0:T(8,128)(2,1)} %param.15) | copy-start | bytes 2359300
  7.2 1.2 copy-start.4
  7.2 7.1 %copy-start.7 = (s32[1,8192]{1,0:T(1,128)S(1)}, s32[1,8192]{1,0:T(1,128)}, u32[]{:S(2)}) copy-start(s32[1,8192]{1,0:T(1,128)} %param.10) | copy-start | bytes 98308
  7.2 7.3 %copy-start.8 = (f32[5,1536]{1,0:T(8,128)S(1)}, f32[5,1536]{1,0:T(8,128)}, u32[]{:S(2)}) copy-start(f32[5,1536]{1,0:T(8,128)} %param.12) | copy-start | bytes 92164
  7.2 82.2 %all-gather.2.cloned.1.call-start = ((), (), s32[]{:S(2)}) async-start(), calls=%async_computation.4 | async-start | bytes 15925248 | tf_op jit(solution)/shard_map/all_gather | solution.py:110
  7.9 649.0 %reduce-scatter.5.cloned.1.call-start = ((), (), s32[]{:S(2)}) async-start(), calls=%async_computation.5 | async-start | bytes 9732096 | tf_op jit(solution)/shard_map/reduce_scatter | solution.py:135
  8.4 6.2 collective-permute-start.1
  10.9 5.8 collective-permute-start
  170.6 3.8 copy-start.9
  171.9 35.8 %collective-permute-start.2 = (bf16[8192,2,48]{0,2,1:T(8,128)(2,1)}, bf16[8192,2,48]{0,2,1:T(8,128)(2,1)}, u32[]{:S(2)}, u32[]{:S(2)}) collective-permute-start(bf16[8192,2,48]{0,2,1:T(8,128)(2,1)} %slice_bitcast_fusion), channel_id=1, source_target_pairs={{0,1},{1,0},{2,3},{3,2},{4,5},{5,4},{6,7},{7,6},{8,9},{9,8},{10,11... | collective-permute-start | bytes 4718600 | tf_op jit(solution)/shard_map/ppermute | solution.py:31
  175.4 1.1 copy-start.3
  218.2 1.6 copy-start.1
  218.2 2.4 copy-start.2
  220.6 2.9 copy-start.5
  321.6 0.9 copy-start.6
  429.3 263.3 %reduce-scatter.7.cloned.1.call-start = ((), (), s32[]{:S(2)}) async-start(), calls=%async_computation.6 | async-start | bytes 884736
Sparse Core Ops, SparseCore 0:
  9.9 79.4 all-gather.1
  429.5 227.4 reduce-scatter.4
  659.5 33.1 reduce-scatter.6
where the time goes:
time: 704 us; the launch traced here: 701 us
  waiting for transfers between devices  361 us (51%)
  local copies, waits for them, and re-layouts  121 us (17%)
  blocking collectives  93.6 us (13%)
  other arithmetic  55.5 us (8%)
  matrix products  36.9 us (5%)
  between operations  14 us (2%)
  loops' own time  11.7 us (2%)
  starting transfers between devices  7.23 us (1%)
    reduce_scatter x1, waiting for transfers between devices, local(): lax.psum_scatter(grad_term, 'tm', scatter_dimension=0, tiled=True)  228 us
    all_gather x1, waiting for transfers between devices, local(): lax.all_gather(w_qkv, 'dp', axis=1, tiled=True)  72.7 us
    all_to_all x1, blocking collectives, local(): lax.all_to_all(arranged, 'tm', split_axis=2, concat_axis=0, tiled=True)  66.5 us
    dynamic_slice x96, local copies, waits for them, and re-layouts, pick_rows(): return lax.dynamic_slice_in_dim(array, start, per_step, 0)  58.5 us
    another operation x1, other arithmetic, local(): attended.reshape(frame_count, 1, piece)  45.2 us
    unnamed x4, waiting for transfers between devices  29.7 us
    ppermute x1, waiting for transfers between devices, swapped(): return lax.ppermute(block, axis, route)  29.1 us
    all_to_all x1, blocking collectives, local(): lax.all_to_all(attended.reshape(frame_count, 1, piece), 'tm', split_axis=...  27.1 us
  transfers between devices with their start and end apart: 6, of which 5 were waited for; matrix products, arithmetic and copies ran while one was open for 1% of the time, Pallas kernels for 0%

commit v1 on v0

--- a/solution.py
+++ b/solution.py
@@ -6,6 +6,12 @@
 
 KER = 5
 STRETCH = 256
+convert_the_lanes = lambda frame_in, axis_name: jnp.concatenate(
+    jax.lax.all_to_all(
+        jnp.stack(jnp.split(frame_in, jax.lax.axis_size(axis_name), 2)), axis_name, 0, 0
+    ),
+    0,
+)
 
 
 def extended(block, sides, width):
@@ -110,7 +116,7 @@
         activ, lax.all_gather(w_qkv, "dp", axis=1, tiled=True), preferred_element_type=jnp.float32
     ).astype(jnp.bfloat16)
     arranged = qkv.reshape(rows, 3, tm_count, piece)
-    arrived = lax.all_to_all(arranged, "tm", split_axis=2, concat_axis=0, tiled=True)
+    arrived = convert_the_lanes(arranged, "tm")
     frame_count = arrived.shape[0]
     lower = lax.axis_index("tm") % 2 == 0
     own_pair = arrived[:, 0:2, 0, :]

time: 704 us -> 704 us (level)
    unnamed x30 -> x59, local copies, waits for them, and re-layouts: 22.9 us -> 21.8 us
  transfers between devices with their start and end apart: 6 -> 6, of which waited for: 5 -> 5; matrix products, arithmetic and copies ran while one was open for 1% -> 2% of each run, Pallas kernels for 0% -> 0%
where the time goes in v1:
time: 704 us; the launch traced here: 701 us
  waiting for transfers between devices  360 us (51%)
  local copies, waits for them, and re-layouts  122 us (17%)
  blocking collectives  93.6 us (13%)
  other arithmetic  55.5 us (8%)
  matrix products  36.9 us (5%)
  between operations  14.3 us (2%)
  loops' own time  11.7 us (2%)
  starting transfers between devices  7.23 us (1%)
    reduce_scatter x1, waiting for transfers between devices, local(): lax.psum_scatter(grad_term, 'tm', scatter_dimension=0, tiled=True)  228 us
    all_gather x1, waiting for transfers between devices, local(): lax.all_gather(w_qkv, 'dp', axis=1, tiled=True)  72.4 us
    all_to_all x1, blocking collectives, jax.lax.all_to_all(jnp.stack(jnp.split(frame_in, jax.lax.axis_size(axis_n...  66.5 us
    dynamic_slice x96, local copies, waits for them, and re-layouts, pick_rows(): return lax.dynamic_slice_in_dim(array, start, per_step, 0)  58.5 us
    another operation x1, other arithmetic, local(): attended.reshape(frame_count, 1, piece)  45.2 us
    unnamed x4, waiting for transfers between devices  29.7 us
    ppermute x1, waiting for transfers between devices, swapped(): return lax.ppermute(block, axis, route)  28.7 us
    all_to_all x1, blocking collectives, local(): lax.all_to_all(attended.reshape(frame_count, 1, piece), 'tm', split_axis=...  27.1 us
  transfers between devices with their start and end apart: 6, of which 5 were waited for; matrix products, arithmetic and copies ran while one was open for 2% of the time, Pallas kernels for 0%

profile of v1, /device:TPU:4, one launch (start us, length us, event | category | flops | bytes accessed | tf_op | source)
XLA Modules:
  0.0 701.1 jit_solution(7414366926172145263)
XLA Ops:
  8.8 2.4 collective-permute-start.1
  11.2 3.4 collective-permute-start
  15.7 1.3 collective-permute-done
  17.0 72.4 %all-gather.2.cloned.1.call-done = bf16[1536,4608]{0,1:T(8,128)(2,1)} async-done(((bf16[1536,576]{0,1:T(8,128)(2,1)}), bf16[1536,4608]{0,1:T(8,128)(2,1)}) %all-gather.2.cloned.1.call-update) | async-done | bytes 14155792 | tf_op jit(solution)/shard_map/all_gather | solution.py:116
  89.4 11.5 %convolution_convert_fusion.1 = bf16[256,4608]{1,0:T(8,128)(2,1)} fusion(bf16[1536,4608]{0,1:T(8,128)(2,1)} %all-gather.2.cloned.1.call-done, bf16[256,1536]{1,0:T(8,128)(2,1)S(1)} %copy-done.3, bf16[2,1536]{1,0:T(2,128)(2,1)S(1)} %collective-permute-done, bf16[258,1536]{1,0:T(8,128)(2,1)S(1)} %constant_dynamic-update-slice_fusion.1, ...), kind=kOutput, calls=%fused_computation.23 | convolution fusion | flops 3636461568 | bytes 18925568 | tf_op jit(solution)/shard_map/dot_general | solution.py:115
  100.8 2.8 copy.116
  104.2 66.5 %all_to_all.20 = bf16[32,256,3,1,48]{1,4,2,3,0:T(8,128)(2,1)S(1)} all-to-all(bf16[32,256,3,1,48]{1,4,2,3,0:T(8,128)(2,1)S(1)} %fusion.29), channel_id=1, replica_groups=mesh['dp'=8,'tm'=32] {'tm'}, dimensions={0} | all-to-all | bytes 4718592 | tf_op jit(solution)/shard_map/all_to_all | solution.py:10
  170.9 1.3 slice_bitcast_fusion
  172.2 1.3 collective-permute-start.2
  175.9 1.8 slice.102
  177.7 1.6 fusion.13
  179.3 28.7 %collective-permute-done.2 = bf16[8192,2,48]{0,2,1:T(8,128)(2,1)} collective-permute-done((bf16[8192,2,48]{0,2,1:T(8,128)(2,1)}, bf16[8192,2,48]{0,2,1:T(8,128)(2,1)}, u32[]{:S(2)}, u32[]{:S(2)}) %collective-permute-start.2) | collective-permute-done | bytes 1572896 | tf_op jit(solution)/shard_map/ppermute | solution.py:37
  208.0 3.8 maximum_select_fusion
  212.1 1.3 slice.119
  213.3 1.6 copy.196
  214.9 3.6 slice.109
  218.5 1.6 copy.195
  220.9 2.9 fusion.11
  223.8 98.1 %while.11 = (s32[]{:T(128)}, bf16[16,512,48]{1,2,0:T(8,128)(2,1)S(1)}, s32[16]{0:T(128)S(1)}, bf16[32,512,1,48]{1,0,3,2:T(8,128)(2,1)}, s32[32,512]{1,0:T(8,128)...) while((s32[]{:T(128)}, ...), condition=%wide.region_3.4_spmd.clone, body=%wide.region_0.3_spmd.clone.sunk | while | flops 77621248 | bytes 3646681 | solution.py:89
  225.1 1.3 constant_dynamic-slice_fusion.12
  226.4 1.1 constant_dynamic-slice_fusion.13
  231.2 1.3 constant_dynamic-slice_fusion.12
  232.5 1.1 constant_dynamic-slice_fusion.13
  237.3 1.3 constant_dynamic-slice_fusion.12
  238.7 1.1 constant_dynamic-slice_fusion.13
  243.5 1.3 constant_dynamic-slice_fusion.12
  244.8 1.1 constant_dynamic-slice_fusion.13
  249.6 1.3 constant_dynamic-slice_fusion.12
  250.9 1.1 constant_dynamic-slice_fusion.13
  255.7 1.3 constant_dynamic-slice_fusion.12
  257.1 1.1 constant_dynamic-slice_fusion.13
  261.9 1.3 constant_dynamic-slice_fusion.12
  263.2 1.1 constant_dynamic-slice_fusion.13
  268.0 1.3 constant_dynamic-slice_fusion.12
  269.3 1.1 constant_dynamic-slice_fusion.13
  274.1 1.3 constant_dynamic-slice_fusion.12
  275.5 1.1 constant_dynamic-slice_fusion.13
  280.3 1.3 constant_dynamic-slice_fusion.12
  281.6 1.1 constant_dynamic-slice_fusion.13
  286.4 1.3 constant_dynamic-slice_fusion.12
  287.7 1.1 constant_dynamic-slice_fusion.13
  292.5 1.3 constant_dynamic-slice_fusion.12
  293.9 1.1 constant_dynamic-slice_fusion.13
  298.7 1.3 constant_dynamic-slice_fusion.12
  300.0 1.1 constant_dynamic-slice_fusion.13
  304.8 1.3 constant_dynamic-slice_fusion.12
  306.1 1.1 constant_dynamic-slice_fusion.13
  310.9 1.3 constant_dynamic-slice_fusion.12
  312.3 1.1 constant_dynamic-slice_fusion.13
  317.1 1.3 constant_dynamic-slice_fusion.12
  318.4 1.1 constant_dynamic-slice_fusion.13
  322.8 2.0 copy.156
  324.8 6.2 reshape.93
  331.5 45.2 %reduce.20 = bf16[8192,48]{1,0:T(8,128)(2,1)S(1)} reduce(bf16[8192,1,48]{2,1,0:T(2,128)(2,1)} %reshape.93, bf16[]{:T(256)} %broadcast.84), dimensions={1}, to_apply=%reshape.93.reduce_sub_computation | reduce | bytes 1572866 | tf_op jit(solution)/shard_map/reshape;reshape | solution.py:134
  376.7 4.2 reshape.111
  380.9 27.1 %all_to_all.21 = bf16[32,2,6144]{2,1,0:T(2,128)(2,1)S(1)} all-to-all(bf16[32,2,6144]{2,1,0:T(2,128)(2,1)} %reshape.111), channel_id=1, replica_groups=mesh['dp'=8,'tm'=32] {'tm'}, dimensions={0} | all-to-all | bytes 1572864 | tf_op jit(solution)/shard_map/all_to_all | solution.py:133
  408.0 7.9 %reshape.112 = bf16[8192,1,48]{2,1,0:T(2,128)(2,1)} reshape(bf16[32,2,6144]{2,1,0:T(2,128)(2,1)S(1)} %all_to_all.21) | data formatting | bytes 1572864
  415.9 8.1 %copy.154 = bf16[8192,1,48]{0,2,1:T(8,128)(2,1)S(1)} copy(bf16[8192,1,48]{2,1,0:T(2,128)(2,1)} %reshape.112) | data formatting | bytes 1572864 | tf_op jit(solution)/shard_map/all_to_all | solution.py:133
  424.6 5.0 fusion.66
  429.7 227.5 %reduce-scatter.5.cloned.1.call-done = f32[48,1536]{1,0:T(8,128)} async-done(((f32[1536,1536]{1,0:T(8,128)}), f32[48,1536]{1,0:T(8,128)}) %reduce-scatter.5.cloned.1.call-update) | async-done | bytes 294928 | tf_op jit(solution)/shard_map/reduce_scatter | solution.py:141
  657.3 2.1 copy.157
  659.4 4.6 convolution_convert_fusion.2
  664.0 28.9 %reduce-scatter.7.cloned.1.call-done = f32[192,48]{1,0:T(8,128)} async-done(((f32[1536,48]{1,0:T(8,128)}), f32[192,48]{1,0:T(8,128)}) %reduce-scatter.7.cloned.1.call-update) | async-done | bytes 36880
  693.0 1.6 copy.158
  (272 shorter events, 55.8 us)
Async XLA Ops:
  7.2 417.5 %copy-start = (bf16[256,1536]{1,0:T(8,128)(2,1)S(1)}, bf16[256,1536]{1,0:T(8,128)(2,1)}, u32[]{:S(2)}) copy-start(bf16[256,1536]{1,0:T(8,128)(2,1)} %param.15) | copy-start | bytes 2359300
  7.2 8.3 %copy-start.3 = (bf16[256,1536]{1,0:T(8,128)(2,1)S(1)}, bf16[256,1536]{1,0:T(8,128)(2,1)}, u32[]{:S(2)}) copy-start(bf16[256,1536]{1,0:T(8,128)(2,1)} %param.9) | copy-start | bytes 2359300
  7.2 8.4 %copy-start.7 = (f32[5,1536]{1,0:T(8,128)S(1)}, f32[5,1536]{1,0:T(8,128)}, u32[]{:S(2)}) copy-start(f32[5,1536]{1,0:T(8,128)} %param.12) | copy-start | bytes 92164
  7.2 82.2 %all-gather.2.cloned.1.call-start = ((), (), s32[]{:S(2)}) async-start(), calls=%async_computation.4 | async-start | bytes 15925248 | tf_op jit(solution)/shard_map/all_gather | solution.py:116
  7.9 649.3 %reduce-scatter.5.cloned.1.call-start = ((), (), s32[]{:S(2)}) async-start(), calls=%async_computation.5 | async-start | bytes 9732096 | tf_op jit(solution)/shard_map/reduce_scatter | solution.py:141
  8.8 6.9 collective-permute-start.1
  11.2 5.8 collective-permute-start
  170.9 3.0 copy-start.6
  170.9 3.8 copy-start.8
  172.2 35.8 %collective-permute-start.2 = (bf16[8192,2,48]{0,2,1:T(8,128)(2,1)}, bf16[8192,2,48]{0,2,1:T(8,128)(2,1)}, u32[]{:S(2)}, u32[]{:S(2)}) collective-permute-start(bf16[8192,2,48]{0,2,1:T(8,128)(2,1)} %slice_bitcast_fusion), channel_id=1, source_target_pairs={{0,1},{1,0},{2,3},{3,2},{4,5},{5,4},{6,7},{7,6},{8,9},{9,8},{10,11... | collective-permute-start | bytes 4718600 | tf_op jit(solution)/shard_map/ppermute | solution.py:37
  218.5 1.6 copy-start.1
  218.5 2.4 copy-start.2
  220.9 2.9 copy-start.4
  321.9 0.9 copy-start.5
  429.7 263.3 %reduce-scatter.7.cloned.1.call-start = ((), (), s32[]{:S(2)}) async-start(), calls=%async_computation.6 | async-start | bytes 884736
Sparse Core Ops, SparseCore 0:
  9.9 79.4 all-gather.1
  429.8 227.4 reduce-scatter.4
  659.8 33.1 reduce-scatter.6
